TPU v7x, 512 devices: a whole 4x4x16 slice. The times are simulated.
512 devices in a mesh: src: 32 (over y, x, core), tm: 16 (over z).
Axes of the slice: x: 4, y: 4, z: 16, core: 2. Of those that a mesh axis runs over, the one named last changes fastest.
Arguments:
- observed: float32 [16, 131072], P(None, ('src', 'tm')), may hold values from -8 to 8
- weight_obs: float32 [16, 131072], P(None, ('src', 'tm')), may hold values from 0.25 to 4
- present: int32 [16, 131072], P(None, ('src', 'tm')), may hold values 0 or 1
- source_partials: float32 [5, 16, 131072], P(None, None, ('src', 'tm')), may hold values from -6 to 6
- attitude_partials: float32 [4, 16, 131072], P(None, None, ('src', 'tm')), may hold values from -6 to 6
- phase: float32 [16, 131072], P(None, ('src', 'tm')), may hold values from 0 to 1
- knot_base: int32 [16, 131072], P(None, ('src', 'tm')), may hold values from 0 to 28
- source_id: int32 [16, 131072], P(None, ('src', 'tm')), may hold values from 0 to 127, as said below
- cal_id: int32 [16, 131072], P(None, ('src', 'tm')), may hold values from 0 to 32767
- attitude: float32 [2048], P('tm'), may hold values from -4 to 4
- calibration: float32 [32768], replicated, may hold values from -4 to 4
Outputs:
- source_params: float32 [5, 65536], P(None, ('src', 'tm'))
- attitude_out: float32 [2048], P('tm')
- calibration_out: float32 [32768], replicated
- residual: float32 [16, 131072], P(None, ('src', 'tm'))
Inputs may be any that keep to these rules, and one draw needn't show every extreme that they name: `source_id`: within each device's block of 256 columns the ids name that device's 128 sources, each of them at least once.
All inputs are finite; a program needn't handle non-finite values. No bound on the sum of `present` on one device may be relied on, other than what follows from the above.
Results may differ from a plain program's by a relative error of at most 0.0003.
Values sent between devices are 32-bit elements; how exact they have to be, the bound alone decides.
A program may use at most 64 MiB of HBM per device.

v0:
```python
import jax
import jax.numpy as jnp
from jax import lax
from jax.sharding import PartitionSpec as P

KNOTS_DEV = 32
SRC_DEV = 128
CAL = 32768
ITERS = 2


PAIRS = [(row_id, col_id) for row_id in range(5) for col_id in range(row_id + 1)]


def spline_terms(phase, attitude_partials):
    other = 1.0 - phase
    square = phase * phase
    cube = square * phase
    basis = [
        other * other * other / 6.0,
        (3.0 * cube - 6.0 * square + 4.0) / 6.0,
        (-3.0 * cube + 3.0 * square + 3.0 * phase + 1.0) / 6.0,
        cube / 6.0,
    ]
    return jnp.stack(
        [
            basis[knot_step] * attitude_partials[channel]
            for knot_step in range(4)
            for channel in range(4)
        ]
    )


def attitude_model(local, terms, knot_base):
    coefficients = lax.all_gather(local, "tm", axis=0, tiled=True)
    blocks, slots = knot_base.shape
    table = coefficients.reshape(blocks, -1, 4)
    knots_count = table.shape[1]
    grid = lax.broadcasted_iota(jnp.int32, (1, knots_count, 1), 1)
    running = jnp.zeros(knot_base.shape, jnp.float32)
    for knot_step in range(4):
        hit = (grid == (knot_base + knot_step)[:, None, :]).astype(jnp.float32)
        picked = jnp.einsum(
            "bkc,bks->bcs",
            table,
            hit,
            precision=lax.Precision.HIGHEST,
            preferred_element_type=jnp.float32,
        )
        for channel in range(4):
            running = running + terms[4 * knot_step + channel] * picked[:, channel, :]
    return running


def small_solve(matrix, right_side):
    extent = len(right_side)
    factor = {}
    for member in range(extent):
        for column in range(member + 1):
            running = matrix[member][column]
            for offset in range(column):
                running = running - factor[member, offset] * factor[column, offset]
            if member == column:
                factor[member, member] = jnp.sqrt(running)
            else:
                factor[member, column] = running / factor[column, column]
    forward = []
    for member in range(extent):
        running = right_side[member]
        for offset in range(member):
            running = running - factor[member, offset] * forward[offset]
        forward.append(running / factor[member, member])
    result = [None] * extent
    for member in reversed(range(extent)):
        running = forward[member]
        for offset in range(member + 1, extent):
            running = running - factor[offset, member] * result[offset]
        result[member] = running / factor[member, member]
    return jnp.stack(result)


def source_solve(ids, count, weighted, source_partials, target):
    products = [
        weighted * source_partials[row_id] * source_partials[col_id] for row_id, col_id in PAIRS
    ]
    products = products + [weighted * source_partials[row_id] * target for row_id in range(5)]
    stacked = jnp.moveaxis(jnp.stack(products), 1, 0)
    owners = lax.broadcasted_iota(jnp.int32, (count, 1), 0)

    def accumulate(total, item):
        values, block_ids = item
        hit = (block_ids[None, :] == owners).astype(jnp.float32)
        added = lax.dot_general(
            values,
            hit,
            (((1,), (1,)), ((), ())),
            precision=lax.Precision.HIGHEST,
            preferred_element_type=jnp.float32,
        )
        return (total + added, None)

    sums, unused = lax.scan(
        accumulate, jnp.zeros((len(products), count), jnp.float32), (stacked, ids)
    )
    entries = {}
    for position, pair in enumerate(PAIRS):
        entry_value = sums[position] + (1.0 if pair[0] == pair[1] else 0.0)
        entries[pair[0], pair[1]] = entry_value
        entries[pair[1], pair[0]] = entry_value
    matrix = [[entries[row_id, col_id] for col_id in range(5)] for row_id in range(5)]
    return small_solve(matrix, [sums[15 + row_id] for row_id in range(5)])


def pick_params(params, ids):
    count = params.shape[1]
    owners = lax.broadcasted_iota(jnp.int32, (count, 1), 0)

    def pick_single(carry, block_ids):
        hit = (block_ids[None, :] == owners).astype(jnp.float32)
        return (
            carry,
            jnp.dot(
                params, hit, precision=lax.Precision.HIGHEST, preferred_element_type=jnp.float32
            ),
        )

    unused, picked = lax.scan(pick_single, 0, ids)
    return jnp.moveaxis(picked, 1, 0)


def spd_solve(matrix, right_side):
    eye = jnp.eye(matrix.shape[-1], dtype=jnp.float32)
    lower = jnp.linalg.cholesky(matrix + eye)
    middle = lax.linalg.triangular_solve(lower, right_side[..., None], left_side=True, lower=True)
    result = lax.linalg.triangular_solve(
        lower, middle, left_side=True, lower=True, transpose_a=True
    )
    return result[..., 0]


def block_normals(terms, knot_base, weighted, resid):
    blocks, slots = knot_base.shape
    spread = jnp.moveaxis(terms.reshape(4, 4, blocks, slots), 2, 0)

    def block_single(item):
        part, base, weights, values = item
        grid = lax.broadcasted_iota(jnp.int32, (KNOTS_DEV, slots), 0)
        design = jnp.zeros((KNOTS_DEV, 4, slots), jnp.float32)
        for knot_step in range(4):
            hit = (grid == base[None, :] + knot_step).astype(jnp.float32)
            design = design + hit[:, None, :] * part[knot_step][None, :, :]
        design = design.reshape(KNOTS_DEV * 4, slots)
        normal = lax.dot_general(
            design * weights[None, :],
            design,
            (((1,), (1,)), ((), ())),
            precision=lax.Precision.HIGHEST,
            preferred_element_type=jnp.float32,
        )
        right = jnp.dot(
            design,
            weights * values,
            precision=lax.Precision.HIGHEST,
            preferred_element_type=jnp.float32,
        )
        return (normal, right)

    return lax.map(block_single, (spread, knot_base, weighted, resid))


def body(
    observed,
    weight_obs,
    present,
    source_partials,
    attitude_partials,
    phase,
    knot_base,
    source_id,
    cal_id,
    attitude,
    calibration,
):
    weighted = present.astype(jnp.float32) * weight_obs
    terms = spline_terms(phase, attitude_partials)
    flat_cal = cal_id.reshape(-1)
    local = attitude
    cal_now = calibration
    params = jnp.zeros((5, SRC_DEV), jnp.float32)
    for sweep in range(ITERS):
        target = observed - attitude_model(local, terms, knot_base) - cal_now[cal_id]
        params = source_solve(source_id, SRC_DEV, weighted, source_partials, target)
        resid = target - jnp.sum(source_partials * pick_params(params, source_id), axis=0)
        normals, rights = block_normals(terms, knot_base, weighted, resid)
        normal, right = (
            lax.psum_scatter(normals, "tm", scatter_dimension=0, tiled=True),
            lax.psum_scatter(rights, "tm", scatter_dimension=0, tiled=True),
        )
        normal, right = lax.psum((normal[0], right[0]), "src")
        local = local + spd_solve(normal, right)
        numer = jax.ops.segment_sum((weighted * resid).reshape(-1), flat_cal, num_segments=CAL)
        denom = jax.ops.segment_sum(weighted.reshape(-1), flat_cal, num_segments=CAL)
        numer, denom = lax.psum((numer, denom), ("src", "tm"))
        cal_now = cal_now + numer / (denom + 1.0)
    final = observed - attitude_model(local, terms, knot_base) - cal_now[cal_id]
    final = final - jnp.sum(source_partials * pick_params(params, source_id), axis=0)
    return (params, local, cal_now, final)


def solution(mesh):
    return jax.shard_map(
        body,
        mesh=mesh,
        in_specs=(
            P(None, ("src", "tm")),
            P(None, ("src", "tm")),
            P(None, ("src", "tm")),
            P(None, None, ("src", "tm")),
            P(None, None, ("src", "tm")),
            P(None, ("src", "tm")),
            P(None, ("src", "tm")),
            P(None, ("src", "tm")),
            P(None, ("src", "tm")),
            P("tm"),
            P(),
        ),
        out_specs=(P(None, ("src", "tm")), P("tm"), P(), P(None, ("src", "tm"))),
        check_vma=False,
    )
```

profile of v0, /device:TPU:1, one launch (start us, length us, event | category | flops | bytes accessed | tf_op | source)
XLA Modules:
  0.0 1516.4 jit_solution(14639042611924822357)
XLA Ops:
  8.1 0.8 constant_dynamic-update-slice_fusion.55
  9.1 0.8 copy-done.6
  11.5 28.8 %all-gather = f32[16,1,128]{2,1,0:T(1,128)S(1)} all-gather(f32[1,1,128]{2,1,0:T(1,128)S(1)} %bitcast.924), channel_id=1, replica_groups=mesh['src'=32,'tm'=16] {'tm'}, dimensions={0}, use_global_device_ids=true | all-gather | bytes 8704 | tf_op jit(solution)/shard_map/all_gather | solution.py:35
  42.6 23.0 %gather_fusion = f32[4096]{0:T(1024)S(1)} fusion(f32[32768]{0:T(1024)S(1)} %copy-done, s32[4096]{0:T(1024)S(1)} %broadcast_clamp_fusion), kind=kCustom, calls=%fused_computation | custom fusion | bytes 49152 | tf_op jit(solution)/shard_map/gather | solution.py:191
  66.5 14.9 while.76
  81.6 13.8 while.74
  82.5 0.7 constant_dynamic-slice_fusion.28
  83.4 0.7 constant_dynamic-slice_fusion.28
  84.2 0.7 constant_dynamic-slice_fusion.28
  85.1 0.7 constant_dynamic-slice_fusion.28
  86.0 0.7 constant_dynamic-slice_fusion.28
  86.8 0.7 constant_dynamic-slice_fusion.28
  87.7 0.7 constant_dynamic-slice_fusion.28
  88.5 0.7 constant_dynamic-slice_fusion.28
  89.4 0.7 constant_dynamic-slice_fusion.28
  90.3 0.7 constant_dynamic-slice_fusion.28
  91.1 0.7 constant_dynamic-slice_fusion.28
  92.0 0.7 constant_dynamic-slice_fusion.28
  92.9 0.7 constant_dynamic-slice_fusion.28
  93.7 0.7 constant_dynamic-slice_fusion.28
  94.6 0.7 constant_dynamic-slice_fusion.28
  95.9 13.7 while.72
  109.6 1.0 copy-done.2
  110.7 22.5 %scatter_custom_fusion = f32[32768]{0:T(1024)} fusion(s32[4096]{0:T(1024)S(1)} %bitcast.917, f32[4096]{0:T(1024)S(1)} %bitcast.920, f32[]{:T(128)} %constant.127.clone.1), kind=kCustom, calls=%fused_computation.204 | custom fusion | flops 4096 | bytes 131076 | tf_op jit(solution)/shard_map/scatter-add | solution.py:201
  133.2 22.5 %scatter_custom_fusion.1 = f32[32768]{0:T(1024)} fusion(s32[4096]{0:T(1024)S(1)} %bitcast.918, f32[4096]{0:T(1024)S(1)} %bitcast.922, f32[]{:T(128)} %constant.127.clone.1), kind=kCustom, calls=%fused_computation.202 | custom fusion | flops 4096 | bytes 131076 | tf_op jit(solution)/shard_map/scatter-add | solution.py:202
  155.8 1.3 dynamic-slice
  157.1 22.6 %all-reduce = f32[16,128]{1,0:T(8,128)S(1)} all-reduce(f32[16,128]{1,0:T(8,128)S(1)} %get-tuple-element.204), channel_id=3, replica_groups=mesh['src'=32,'tm'=16] {'tm'}, use_global_device_ids=true, to_apply=%region_11.13.clone | all-reduce | flops 2048 | bytes 16384
  180.4 75.4 %psum.53 = f32[128,1]{0,1:T(1,128)S(1)} all-reduce(f32[128,1]{0,1:T(1,128)S(1)} %fusion.181), channel_id=1, replica_groups=mesh['src'=32,'tm'=16] {'src'}, use_global_device_ids=true, to_apply=%region_12.14 | all-reduce | flops 128 | bytes 1024 | tf_op jit(solution)/shard_map/psum | solution.py:199
  256.1 359.4 %all-reduce.14.cloned.1.call-done = (f32[32768]{0:T(1024)}, f32[32768]{0:T(1024)}) async-done(((f32[32768]{0:T(1024)}, f32[32768]{0:T(1024)}), (f32[32768]{0:T(1024)}, f32[32768]{0:T(1024)})) %all-reduce.14.cloned.1.call-update) | async-done | bytes 262160 | tf_op jit(solution)/shard_map/psum | solution.py:203
  615.5 1.0 divide_add_fusion.1
  616.5 23.0 %gather_fusion.1 = f32[4096]{0:T(1024)S(1)} fusion(f32[32768]{0:T(1024)S(1)} %divide_add_fusion.1, s32[4096]{0:T(1024)S(1)} %broadcast_clamp_fusion), kind=kCustom, calls=%fused_computation.1 | custom fusion | bytes 49152 | tf_op jit(solution)/shard_map/gather | solution.py:191
  639.5 102.1 %all-reduce.8.cloned.1.call-done = f32[128,128]{0,1:T(8,128)} async-done(((f32[128,128]{0,1:T(8,128)}), f32[128,128]{0,1:T(8,128)}) %all-reduce.8.cloned.1.call-update) | async-done | bytes 65552 | tf_op jit(solution)/shard_map/psum | solution.py:199
  741.6 0.9 convert_add_fusion.1
  742.5 0.7 copy-done.8
  743.3 11.7 cholesky.44
  756.3 9.8 custom-call.13
  766.5 22.8 %all-gather.1 = f32[16,1,128]{2,1,0:T(1,128)S(1)} all-gather(f32[1,1,128]{2,1,0:T(1,128)S(1)} %bitcast.923), channel_id=1, replica_groups=mesh['src'=32,'tm'=16] {'tm'}, dimensions={0}, use_global_device_ids=true | all-gather | bytes 8704 | tf_op jit(solution)/shard_map/all_gather | solution.py:35
  791.0 14.9 while.77
  806.1 13.8 while.75
  806.9 0.7 constant_dynamic-slice_fusion.29
  807.8 0.7 constant_dynamic-slice_fusion.29
  808.7 0.7 constant_dynamic-slice_fusion.29
  809.5 0.7 constant_dynamic-slice_fusion.29
  810.4 0.7 constant_dynamic-slice_fusion.29
  811.3 0.7 constant_dynamic-slice_fusion.29
  812.1 0.7 constant_dynamic-slice_fusion.29
  813.0 0.7 constant_dynamic-slice_fusion.29
  813.9 0.7 constant_dynamic-slice_fusion.29
  814.7 0.7 constant_dynamic-slice_fusion.29
  816.5 0.7 constant_dynamic-slice_fusion.29
  820.6 13.7 while.73
  834.4 1.0 copy-done.3
  835.4 22.5 %scatter_custom_fusion.2 = f32[32768]{0:T(1024)} fusion(s32[4096]{0:T(1024)S(1)} %bitcast.919, f32[4096]{0:T(1024)S(1)} %bitcast.921, f32[]{:T(128)} %constant.127.clone.1), kind=kCustom, calls=%fused_computation.200 | custom fusion | flops 4096 | bytes 131076 | tf_op jit(solution)/shard_map/scatter-add | solution.py:201
  858.0 23.2 %all-reduce.1 = f32[16,128]{1,0:T(8,128)S(1)} all-reduce(f32[16,128]{1,0:T(8,128)S(1)} %get-tuple-element.208), channel_id=5, replica_groups=mesh['src'=32,'tm'=16] {'tm'}, use_global_device_ids=true, to_apply=%region_26.30.clone | all-reduce | flops 2048 | bytes 16384
  881.9 75.7 %psum.57 = f32[128,1]{0,1:T(1,128)S(1)} all-reduce(f32[128,1]{0,1:T(1,128)S(1)} %fusion.182), channel_id=1, replica_groups=mesh['src'=32,'tm'=16] {'src'}, use_global_device_ids=true, to_apply=%region_27.31 | all-reduce | flops 128 | bytes 1024 | tf_op jit(solution)/shard_map/psum | solution.py:199
  957.7 380.5 %all-reduce.12.cloned.1.call-done = f32[32768]{0:T(1024)} async-done(((f32[32768]{0:T(1024)}), f32[32768]{0:T(1024)}) %all-reduce.12.cloned.1.call-update) | async-done | bytes 131088 | tf_op jit(solution)/shard_map/psum | solution.py:203
  1338.2 0.9 divide_add_fusion
  1339.1 23.0 %gather_fusion.2 = f32[4096]{0:T(1024)S(1)} fusion(f32[32768]{0:T(1024)S(1)} %divide_add_fusion, s32[4096]{0:T(1024)S(1)} %broadcast_clamp_fusion), kind=kCustom, calls=%fused_computation.2 | custom fusion | bytes 49152 | tf_op jit(solution)/shard_map/gather | solution.py:205
  1362.2 96.1 %all-reduce.10.cloned.1.call-done = f32[128,128]{0,1:T(8,128)} async-done(((f32[128,128]{0,1:T(8,128)}), f32[128,128]{0,1:T(8,128)}) %all-reduce.10.cloned.1.call-update) | async-done | bytes 65552 | tf_op jit(solution)/shard_map/psum | solution.py:199
  1458.3 0.9 convert_add_fusion
  1459.3 0.7 copy-done.9
  1460.0 11.7 cholesky.55
  1473.1 9.8 custom-call.15
  1483.8 22.7 %all-gather.2 = f32[16,1,128]{2,1,0:T(1,128)S(1)} all-gather(f32[1,1,128]{2,1,0:T(1,128)S(1)} %bitcast.925), channel_id=1, replica_groups=mesh['src'=32,'tm'=16] {'tm'}, dimensions={0}, use_global_device_ids=true | all-gather | bytes 8704 | tf_op jit(solution)/shard_map/all_gather | solution.py:35
  (677 shorter events, 77.8 us)
Async XLA Ops:
  8.0 0.9 copy-start.5
  8.0 247.8 %reduce-scatter.3.cloned.1.call-start = ((), (), s32[]{:S(2)}) async-start(), calls=%async_computation.2 | async-start | bytes 1114112 | tf_op jit(solution)/shard_map/reduce_scatter | solution.py:196
  9.0 0.8 copy-start.6
  9.1 0.8 copy-start.4
  10.2 0.7 copy-start.12
  10.9 0.7 copy-start.14
  41.7 0.7 copy-start.11
  41.7 0.9 copy-start
  65.7 0.7 copy-start.10
  109.6 1.0 copy-start.2
  110.6 504.9 %all-reduce.14.cloned.1.call-start = ((), (), s32[]{:S(2)}) async-start(), calls=%async_computation.7 | async-start | bytes 524288 | tf_op jit(solution)/shard_map/psum | solution.py:203
  155.8 585.8 %all-reduce.8.cloned.1.call-start = ((), (), s32[]{:S(2)}) async-start(), calls=%async_computation.3 | async-start | bytes 131072 | tf_op jit(solution)/shard_map/psum | solution.py:199
  255.9 701.8 %reduce-scatter.5.cloned.1.call-start = ((), (), s32[]{:S(2)}) async-start(), calls=%async_computation.4 | async-start | bytes 1114112 | tf_op jit(solution)/shard_map/reduce_scatter | solution.py:196
  742.4 0.8 copy-start.8
  819.9 0.6 copy-start.13
  834.4 1.0 copy-start.3
  835.4 502.8 %all-reduce.12.cloned.1.call-start = ((), (), s32[]{:S(2)}) async-start(), calls=%async_computation.6 | async-start | bytes 262144 | tf_op jit(solution)/shard_map/psum | solution.py:203
  858.0 480.2 %copy-start.7 = (f32[32768]{0:T(1024)S(1)}, f32[32768]{0:T(1024)}, u32[]{:S(2)}) copy-start(f32[32768]{0:T(1024)} %get-tuple-element.348) | copy-start | bytes 393220
  881.2 577.1 %all-reduce.10.cloned.1.call-start = ((), (), s32[]{:S(2)}) async-start(), calls=%async_computation.5 | async-start | bytes 131072 | tf_op jit(solution)/shard_map/psum | solution.py:199
  1339.1 23.1 %copy-start.1 = (f32[32768]{0:T(1024)}, f32[32768]{0:T(1024)S(1)}, u32[]{:S(2)}) copy-start(f32[32768]{0:T(1024)S(1)} %divide_add_fusion) | copy-start | bytes 393220
  1459.1 0.8 copy-start.9
  1483.2 0.6 copy-start.15
Sparse Core Ops, SparseCore 0:
  110.7 63.8 reduce-scatter.2
  835.5 62.7 reduce-scatter.4
Sparse Core Ops, SparseCore 1:
  155.9 459.5 all-reduce.13
  618.6 122.9 all-reduce.7
  881.3 456.8 all-reduce.11
  1341.8 116.4 all-reduce.9
where the time goes:
time: 1530 us; the launch traced here: 1520 us
  waiting for transfers between devices  938 us (61%)
  blocking collectives  271 us (18%)
  local copies, waits for them, and re-layouts  134 us (9%)
  other arithmetic  123 us (8%)
  matrix products  28.4 us (2%)
  between operations  16.6 us (1%)
    psum x2, waiting for transfers between devices, body(): numer, denom = lax.psum((numer, denom), ('src', 'tm'))  740 us
    psum x2, waiting for transfers between devices, body(): normal, right = lax.psum((normal[0], right[0]), 'src')  198 us
    psum x2, blocking collectives, body(): normal, right = lax.psum((normal[0], right[0]), 'src')  151 us
    all_gather x3, blocking collectives, attitude_model(): coefficients = lax.all_gather(local, 'tm', axis=0, tiled=True)  74.3 us
    dynamic_slice x96, local copies, waits for them, and re-layouts, source_solve(): lax.scan(accumulate, jnp.zeros((len(products), count), jnp.float32), (sta...  46.8 us
    gather x4, local copies, waits for them, and re-layouts, body(): cal_now[cal_id]  46.1 us
    unnamed x2, blocking collectives  45.9 us
    scatter-add x2, other arithmetic, body(): jax.ops.segment_sum((weighted * resid).reshape(-1), flat_cal, num_segment...  45 us
  transfers between devices with their start and end apart: 6, of which 4 were waited for; matrix products, arithmetic and copies ran while one was open for 8% of the time, Pallas kernels for 0%

commit v1 on v0

v1 whole, which is shorter than its diff:
```python
import functools

import jax
import jax.numpy as jnp
from jax import lax
from jax.experimental import pallas as pl
from jax.experimental.pallas import tpu as pltpu
from jax.sharding import PartitionSpec as P

MESH = pl.DeviceIdType.MESH
F32, BF16 = jnp.float32, jnp.bfloat16
ROWS, SLOT, SRC, KNOTS, LANES = 16, 256, 128, 32, 128
OBS = ROWS * SLOT
SHARD = 8
PAIRS = [(i, j) for i in range(5) for j in range(i + 1)]
TILES = [(i, h) for i in range(2) for h in range(2)]
NT = (((1,), (1,)), ((), ()))


def iota(shape, axis):
    return lax.broadcasted_iota(jnp.int32, shape, axis)


def loop(count, step, unroll=1):
    def body(at, carry):
        step(at)
        return carry

    lax.fori_loop(0, count, body, 0, unroll=unroll)


def split(value):
    head = value.astype(BF16).astype(F32)
    return head, value - head


def nt_dot(left, right):
    return lax.dot_general(left, right, NT, preferred_element_type=F32)


def whole(tiles):
    return jnp.concatenate(
        [jnp.concatenate([tiles[i, 0], tiles[i, 1]], axis=1) for i in range(2)], axis=0
    )


def tile(ref, i, h):
    return ref[8 * i : 8 * i + 8, 128 * h : 128 * h + 128]


def along(table, places):
    return jnp.take_along_axis(table, places, axis=1)


def wide(row, rows=8):
    return jnp.broadcast_to(row, (rows, row.shape[-1]))


def choose(rows, order):
    place = iota((8, rows[0].shape[-1]), 0)
    out = wide(rows[order[0]])
    for r in range(1, 8):
        if order[r] != order[r - 1]:
            out = jnp.where(place >= r, wide(rows[order[r]]), out)
    return out


def factor_of(entries):
    low, inv = {}, {}
    for i in range(5):
        for j in range(i + 1):
            rest = entries[i, j]
            for o in range(j):
                rest = rest - low[i, o] * low[j, o]
            if i == j:
                inv[i] = 1.0 / jnp.sqrt(rest)
            else:
                low[i, j] = rest * inv[j]
    return low, inv


def solve_with(low, inv, right):
    forward = []
    for i in range(5):
        rest = right[i]
        for o in range(i):
            rest = rest - low[i, o] * forward[o]
        forward.append(rest * inv[i])
    out = [None] * 5
    for i in reversed(range(5)):
        rest = forward[i]
        for o in range(i + 1, 5):
            rest = rest - low[o, i] * out[o]
        out[i] = rest * inv[i]
    return out


def band_place(shape):
    lane = iota(shape, 1)
    return iota(shape, 0) + 32 * (lane // 32) + lane % 4


def kernel(
    ns,
    nt,
    obs,
    wobs,
    pres,
    sp,
    ap,
    ph,
    kb,
    sid,
    cid,
    att,
    cal,
    params_o,
    att_o,
    cal_o,
    res_o,
    rows_s,
    dd,
    hot_hi,
    hot_src,
    units,
    lhs,
    matrix,
    fac,
    inv_den,
    qbuf,
    qsend,
    a1s,
    a1r,
    b1s,
    b1r,
    pair_r,
    a2s,
    a2r,
    b2s,
    b2r,
    c2s,
    c2r,
    a3s,
    a3r,
    b3s,
    b3r,
    c3s,
    c3r,
    send,
    recv,
):
    me_s, me_t = lax.axis_index("src"), lax.axis_index("tm")

    def to_src(stage, source, target, other, sender):
        return pltpu.make_async_remote_copy(
            src_ref=source,
            dst_ref=target,
            send_sem=send.at[stage, other],
            recv_sem=recv.at[stage, sender],
            device_id=(other, me_t),
            device_id_type=MESH,
        )

    def to_tm(stage, source, target, other, sender):
        return pltpu.make_async_remote_copy(
            src_ref=source,
            dst_ref=target,
            send_sem=send.at[stage, other],
            recv_sem=recv.at[stage, sender],
            device_id=(me_s, other),
            device_id_type=MESH,
        )

    def others(count, me, step):
        def body(d, carry):
            step(lax.rem(me + d, count))
            return carry

        lax.fori_loop(1, count, body, 0)

    def scatter_start(stage, source, target):
        others(
            ns, me_s, lambda o: to_src(stage, source.at[o], target.at[me_s], o, me_s).start()
        )
        target[me_s] = source[me_s]

    def scatter_wait(stage, source, target):
        def step(o):
            copy = to_src(stage, source.at[o], target.at[o], o, o)
            copy.wait_recv()

        others(ns, me_s, step)

    def scatter_sent(stage, source, target):
        others(
            ns,
            me_s,
            lambda o: to_src(stage, source.at[o], target.at[me_s], o, me_s).wait_send(),
        )

    def gather_start(stage, source, target, axis):
        count, me, to = (ns, me_s, to_src) if axis == "src" else (nt, me_t, to_tm)
        others(count, me, lambda o: to(stage, source, target.at[me], o, me).start())
        target[me] = source[...]

    def gather_wait(stage, source, target, axis):
        count, me, to = (ns, me_s, to_src) if axis == "src" else (nt, me_t, to_tm)
        others(count, me, lambda o: to(stage, source, target.at[o], o, o).wait_recv())

    def gather_sent(stage, source, target, axis):
        count, me, to = (ns, me_s, to_src) if axis == "src" else (nt, me_t, to_tm)
        others(count, me, lambda o: to(stage, source, target.at[me], o, me).wait_send())

    barrier = pltpu.get_barrier_semaphore()

    def greet_src(o):
        pl.semaphore_signal(barrier, inc=1, device_id=(o, me_t), device_id_type=MESH)

    def greet_tm(o):
        pl.semaphore_signal(barrier, inc=1, device_id=(me_s, o), device_id_type=MESH)

    others(ns, me_s, greet_src)
    others(nt, me_t, greet_tm)

    weight = pres[...].astype(F32) * wobs[...]
    root = jnp.sqrt(weight)
    u = ph[...]
    square = u * u
    cube = square * u
    other = 1.0 - u
    basis = [
        other * other * other / 6.0,
        (3.0 * cube - 6.0 * square + 4.0) / 6.0,
        (-3.0 * cube + 3.0 * square + 3.0 * u + 1.0) / 6.0,
        cube / 6.0,
    ]
    for j in range(4):
        rows_s[j] = basis[j] * root
        rows_s[4 + j] = basis[j]
    rows_s[8] = weight
    rows_s[9] = root
    w_hi, w_lo = split(weight)
    rows_s[10] = w_hi
    rows_s[11] = w_lo

    def row(at, k):
        return rows_s[at, pl.ds(k, 1), :]

    def lanes(k):
        return pl.ds(pl.multiple_of(k * SLOT, SLOT), SLOT)

    spread = band_place((ROWS, LANES))
    group = (iota((ROWS, LANES), 1) % 32) // 4

    def design_row(k):
        knot = iota((KNOTS, SLOT), 0) - wide(kb[pl.ds(k, 1), :], KNOTS)
        share = jnp.zeros((KNOTS, SLOT), F32)
        for j in range(4):
            share = jnp.where(knot == j, wide(row(j, k), KNOTS), share)
        for c in range(4):
            value = share * wide(ap[c, pl.ds(k, 1), :], KNOTS)
            head, tail = split(value)
            dd[k, 32 * c : 32 * c + 32, :] = head.astype(BF16)
            dd[k, 128 + 32 * c : 160 + 32 * c, :] = tail.astype(BF16)
        both = dd[k]
        full = nt_dot(both, both)
        normal = full[:128, :128] + full[:128, 128:] + full[128:, :128] + full[128:, 128:]
        packed = jnp.zeros((ROWS, LANES), F32)
        for g in range(8):
            part = along(normal[16 * g : 16 * g + 16], (spread + 16 * g) & 127)
            packed = jnp.where(group == g, part, packed)
        a1s[2 * k, 8:16, :] = packed[:8]
        a1s[2 * k + 1, 8:16, :] = packed[8:]

    loop(ROWS, design_row)

    def hot_row(k):
        ids = cid[pl.ds(k, 1), :]
        hit = iota((256, SLOT), 0) == wide(lax.shift_right_logical(ids, 7), 256)
        hot_hi[:, lanes(k)] = jnp.where(hit, 1.0, 0.0).astype(BF16)
        hit = iota((SRC, SLOT), 0) == wide(sid[pl.ds(k, 1), :], SRC)
        hot_src[:, lanes(k)] = jnp.where(hit, 1.0, 0.0).astype(BF16)

    loop(ROWS, hot_row)

    def unit_sums():
        def unit_row(k):
            low = cid[pl.ds(k, 1), :] & 127
            hit = iota((LANES, SLOT), 0) == wide(low, LANES)
            units[:128, lanes(k)] = jnp.where(hit, wide(row(10, k), LANES), 0.0).astype(BF16)
            units[128:, lanes(k)] = jnp.where(hit, wide(row(11, k), LANES), 0.0).astype(BF16)

        loop(ROWS, unit_row)
        both = nt_dot(hot_hi[...], units[...])
        return both[:, :128] + both[:, 128:]

    sums = unit_sums()
    for s in range(ns):
        a1s[s, 0:8, :] = sums[8 * s : 8 * s + 8]

    to_channel = iota((8, LANES), 1)
    to_channel = 4 * (to_channel % 32) + to_channel // 32
    qsend[...] = along(wide(att[...]), to_channel)[0:1]

    pl.semaphore_wait(barrier, ns + nt - 2)
    gather_start(0, qsend, qbuf, "tm")
    scatter_start(1, a1s, a1r)

    def source_row(k):
        a = [sp[i, pl.ds(k, 1), :] for i in range(5)]
        w = row(8, k)
        parts = []
        for first in (0, 8):
            chosen = (PAIRS + [(4, 4)])[first : first + 8]
            left = choose(a, [p[0] for p in chosen])
            parts.append(left * choose(a, [p[1] for p in chosen]) * wide(w))
        value = jnp.concatenate(parts, axis=0)
        head, tail = split(value)
        lhs[:16, lanes(k)] = head.astype(BF16)
        lhs[16:, lanes(k)] = tail.astype(BF16)

    loop(ROWS, source_row)
    sums = nt_dot(lhs[...], hot_src[...])
    sums = sums[:16] + sums[16:]
    entries = {}
    for at, (i, j) in enumerate(PAIRS):
        entries[i, j] = sums[at : at + 1] + (1.0 if i == j else 0.0)
    low, inv = factor_of(entries)
    keep = [low[i, j] for i, j in PAIRS if i != j] + [inv[i] for i in range(5)]
    for at, value in enumerate(keep):
        fac[at : at + 1] = value

    scatter_wait(1, a1s, a1r)
    b1s[...] = jnp.sum(a1r[...], axis=0)
    gather_start(2, b1s, b1r, "tm")

    def remaining(table, cal_tile):
        first = {t: jnp.zeros((8, LANES), F32) for t in TILES}
        low_id = {t: tile(cid, *t) & 127 for t in TILES}
        high_id = {t: lax.shift_right_logical(tile(cid, *t), 7) for t in TILES}

        def step(at, carry):
            carry = dict(zip(TILES, carry))
            block = cal_tile(at)
            for r in range(8):
                line = wide(block[r : r + 1])
                for t in TILES:
                    carry[t] = jnp.where(
                        high_id[t] == 8 * at + r, along(line, low_id[t]), carry[t]
                    )
            return tuple(carry[t] for t in TILES)

        got = lax.fori_loop(0, 32, step, tuple(first[t] for t in TILES))
        out = {}
        for t, offset in zip(TILES, got):
            i, h = t
            base = tile(kb, i, h)
            model = jnp.zeros((8, LANES), F32)
            for j in range(4):
                sum_c = jnp.zeros((8, LANES), F32)
                for c in range(4):
                    part = along(table[8 * i : 8 * i + 8], base + (32 * c + j))
                    sum_c = sum_c + tile(ap.at[c], i, h) * part
                model = model + tile(rows_s.at[4 + j], i, h) * sum_c
            out[t] = tile(obs, i, h) - model - offset
        return out

    def less_sources(target, params):
        out = {}
        for t in TILES:
            ids = tile(sid, *t)
            total = jnp.zeros((8, LANES), F32)
            for i in range(5):
                total = total + tile(sp.at[i], *t) * along(wide(params[i]), ids)
            out[t] = target[t] - total
        return out

    def solve_sources(target):
        rows_s[12] = rows_s[8] * whole(target)

        def side_row(k):
            a = [sp[i, pl.ds(k, 1), :] for i in range(5)]
            value = choose(a, [0, 1, 2, 3, 4, 4, 4, 4]) * wide(row(12, k))
            head, tail = split(value)
            lhs[:16, lanes(k)] = jnp.concatenate([head, tail], axis=0).astype(BF16)

        loop(ROWS, side_row)
        sums = nt_dot(lhs[:16, :], hot_src[...])
        sums = sums[:8] + sums[8:]
        kept = [fac[at : at + 1] for at in range(15)]
        low = dict(zip([p for p in PAIRS if p[0] != p[1]], kept[:10]))
        return solve_with(low, kept[10:], [sums[i : i + 1] for i in range(5)])

    def right_sides(resid, out):
        resid = whole(resid)
        value = rows_s[8] * resid
        head, tail = split(value)
        rows_s[10] = head
        rows_s[11] = tail
        sums = unit_sums()
        for s in range(ns):
            out[s, 0:8, :] = sums[8 * s : 8 * s + 8]
        head, tail = split(rows_s[9] * resid)
        left = jnp.concatenate([head, tail], axis=0).astype(BF16)
        for k in range(ROWS):
            got = nt_dot(left, dd[k])
            got = got[:, :128] + got[:, 128:]
            got = got[k : k + 1] + got[16 + k : 17 + k]
            out[2 * k, 8:9, :] = got
            out[2 * k + 1, 8:9, :] = got

    gather_wait(0, qsend, qbuf, "tm")
    table = jnp.concatenate([qbuf[k] for k in range(nt)], axis=0)
    target = remaining(table, lambda at: cal[pl.ds(pl.multiple_of(8 * at, 8), 8), :])
    params = solve_sources(target)
    right_sides(less_sources(target, params), a2s)
    scatter_start(3, a2s, a2r)

    gather_wait(2, b1s, b1r, "tm")
    summed = jnp.sum(b1r[...], axis=0)
    inv_den[...] = 1.0 / (1.0 + summed[0:8])
    half = lax.rem(me_s, 2)
    owned = me_s // 2
    b1s_sent = lambda: gather_sent(2, b1s, b1r, "tm")
    pair_r[half] = summed[8:16]
    partner = me_s + 1 - 2 * half
    swap = pltpu.make_async_remote_copy(
        src_ref=pair_r.at[half],
        dst_ref=pair_r.at[half],
        send_sem=send.at[9, 0],
        recv_sem=recv.at[9, 0],
        device_id=(partner, me_t),
        device_id_type=MESH,
    )
    swap.start()

    scatter_wait(3, a2s, a2r)
    b2s[...] = jnp.sum(a2r[...], axis=0)
    gather_start(4, b2s, b2r, "tm")

    swap.wait()
    packed = jnp.concatenate([pair_r[0], pair_r[1]], axis=0)
    lane = iota((ROWS, LANES), 1)
    for g in range(8):
        index = iota((ROWS, LANES), 0) + 16 * g
        ahead = (lane - index) & 127
        place = 32 * (ahead // 32) + 4 * g + ahead % 4
        matrix[16 * g : 16 * g + 16, :] = jnp.where(ahead % 32 < 4, along(packed, place), 0.0)
    upper = matrix[...]
    r_id, c_id = iota((128, 128), 0), iota((128, 128), 1)
    strict = jnp.where(r_id % 32 == c_id % 32, 0.0, upper)
    matrix[...] = upper + strict.T + jnp.where(r_id == c_id, 1.0, 0.0)

    def eliminate(i, carry):
        line = matrix[pl.ds(i, 1), :]
        here = iota((8, LANES), 1) == i
        at = jnp.zeros((8, LANES), jnp.int32) + i
        line = wide(line)
        pivot = 1.0 / along(line, at)
        scaled = jnp.where(here, pivot, line * pivot)
        for g in range(16):
            block = matrix[8 * g : 8 * g + 8, :]
            matrix[8 * g : 8 * g + 8, :] = jnp.where(here, 0.0, block) - along(block, at) * scaled
        matrix[pl.ds(i, 1), :] = scaled[0:1]
        return carry

    lax.fori_loop(0, 128, eliminate, 0)

    own_cal = pl.ds(pl.multiple_of(8 * me_s, 8), 8)

    def advance(now, later, offsets, q):
        got = jnp.sum(now[...], axis=0)
        later[0:8, :] = offsets + got[0:8] * inv_den[...]
        step = jnp.dot(
            wide(got[8:9]), matrix[...], precision=lax.Precision.HIGHEST, preferred_element_type=F32
        )
        later[8:9, :] = q + step[0:1]

    gather_wait(4, b2s, b2r, "tm")
    advance(b2r, c2s, cal[own_cal, :], qbuf[owned])
    gather_start(5, c2s, c2r, "src")
    gather_wait(5, c2s, c2r, "src")

    def table_of(got):
        return jnp.concatenate([got[2 * k, 8:9, :] for k in range(nt)], axis=0)

    target = remaining(table_of(c2r), lambda at: c2r[at, 0:8, :])
    params = solve_sources(target)
    for i in range(5):
        params_o[i : i + 1, :] = params[i]
    right_sides(less_sources(target, params), a3s)
    scatter_start(6, a3s, a3r)
    scatter_wait(6, a3s, a3r)
    b3s[...] = jnp.sum(a3r[...], axis=0)
    gather_start(7, b3s, b3r, "tm")
    gather_wait(7, b3s, b3r, "tm")
    advance(b3r, c3s, c2s[0:8, :], c2s[8:9, :])
    gather_start(8, c3s, c3r, "src")
    gather_wait(8, c3s, c3r, "src")

    table = table_of(c3r)
    target = remaining(table, lambda at: c3r[at, 0:8, :])
    res_o[...] = whole(less_sources(target, params))
    for s in range(ns):
        cal_o[8 * s : 8 * s + 8, :] = c3r[s, 0:8, :]
    to_knot = iota((8, LANES), 1)
    to_knot = 32 * (to_knot % 4) + to_knot // 4
    att_o[...] = along(wide(c3r[2 * me_t, 8:9, :]), to_knot)[0:1]

    gather_sent(0, qsend, qbuf, "tm")
    scatter_sent(1, a1s, a1r)
    gather_sent(2, b1s, b1r, "tm")
    scatter_sent(3, a2s, a2r)
    gather_sent(4, b2s, b2r, "tm")
    gather_sent(5, c2s, c2r, "src")
    scatter_sent(6, a3s, a3r)
    gather_sent(7, b3s, b3r, "tm")
    gather_sent(8, c3s, c3r, "src")


def body(ns, nt, *arrays):
    *arrays, attitude, calibration = arrays
    vmem = pl.BlockSpec(memory_space=pltpu.VMEM)
    shard = SHARD + 1
    iteration = [
        pltpu.VMEM((ns, shard, LANES), F32),
        pltpu.VMEM((ns, shard, LANES), F32),
        pltpu.VMEM((shard, LANES), F32),
        pltpu.VMEM((nt, shard, LANES), F32),
        pltpu.VMEM((shard, LANES), F32),
        pltpu.VMEM((ns, shard, LANES), F32),
    ]
    params, att, cal, resid = pl.pallas_call(
        functools.partial(kernel, ns, nt),
        out_shape=(
            jax.ShapeDtypeStruct((5, SRC), F32),
            jax.ShapeDtypeStruct((1, LANES), F32),
            jax.ShapeDtypeStruct((256, LANES), F32),
            jax.ShapeDtypeStruct((ROWS, SLOT), F32),
        ),
        in_specs=[vmem] * 11,
        out_specs=(vmem,) * 4,
        scratch_shapes=[
            pltpu.VMEM((13, ROWS, SLOT), F32),
            pltpu.VMEM((ROWS, 256, SLOT), BF16),
            pltpu.VMEM((256, OBS), BF16),
            pltpu.VMEM((SRC, OBS), BF16),
            pltpu.VMEM((256, OBS), BF16),
            pltpu.VMEM((32, OBS), BF16),
            pltpu.VMEM((128, 128), F32),
            pltpu.VMEM((16, LANES), F32),
            pltpu.VMEM((8, LANES), F32),
            pltpu.VMEM((nt, 1, LANES), F32),
            pltpu.VMEM((1, LANES), F32),
            pltpu.VMEM((ns, 16, LANES), F32),
            pltpu.VMEM((ns, 16, LANES), F32),
            pltpu.VMEM((16, LANES), F32),
            pltpu.VMEM((nt, 16, LANES), F32),
            pltpu.VMEM((2, 8, LANES), F32),
            *iteration,
            *iteration,
            pltpu.SemaphoreType.DMA((10, ns)),
            pltpu.SemaphoreType.DMA((10, ns)),
        ],
        compiler_params=pltpu.CompilerParams(
            collective_id=0, has_side_effects=True, vmem_limit_bytes=40 * 2**20
        ),
        name="astrometric",
    )(*arrays, attitude.reshape(1, LANES), calibration.reshape(256, LANES))
    return params, att.reshape(LANES), cal.reshape(-1), resid


def solution(mesh):
    spread = P(None, ("src", "tm"))
    return jax.shard_map(
        functools.partial(body, mesh.shape["src"], mesh.shape["tm"]),
        mesh=mesh,
        in_specs=(
            spread,
            spread,
            spread,
            P(None, None, ("src", "tm")),
            P(None, None, ("src", "tm")),
            spread,
            spread,
            spread,
            spread,
            P("tm"),
            P(),
        ),
        out_specs=(spread, P("tm"), P(), spread),
        check_vma=False,
    )
```

time: 1530 us -> 111 us (0.07)
  waiting for transfers between devices: 938 us -> 0 us
  blocking collectives: 271 us -> 0 us
  local copies, waits for them, and re-layouts: 134 us -> 10.7 us
  other arithmetic: 123 us -> 0 us
  Pallas kernels: 0 us -> 99.3 us
  matrix products: 28.4 us -> 0 us
  between operations: 16.6 us -> 0.66 us
    psum x4 -> x0, waiting for transfers between devices: 938 us -> none  [the longest x2 740 us: body(): numer, denom = lax.psum((numer, denom), ('src', 'tm'))]
    psum x2 -> x0, blocking collectives: 151 us -> none  [body(): normal, right = lax.psum((normal[0], right[0]), 'src')]
    pallas_call x0 -> x1, Pallas kernels: none -> 99.3 us  [body(): pl.pallas_call(functools.partial(kernel, ns, nt), out_shape=(jax.ShapeDty...]
    all_gather x3 -> x0, blocking collectives: 74.3 us -> none  [attitude_model(): coefficients = lax.all_gather(local, 'tm', axis=0, tiled=True)]
    gather x6 -> x0, local copies, waits for them, and re-layouts: 69.1 us -> none  [the longest x4 46.1 us: body(): cal_now[cal_id]]
    scatter-add x3 -> x0, other arithmetic: 67.6 us -> none  [the longest x2 45 us: body(): jax.ops.segment_sum((weighted * resid).reshape(-1), flat_cal, num_segment...]
    dynamic_slice x128 -> x0, local copies, waits for them, and re-layouts: 47.2 us -> none  [the longest x96 46.8 us: source_solve(): lax.scan(accumulate, jnp.zeros((len(products), count), jnp.float32), (sta...]
    unnamed x2 -> x0, blocking collectives: 45.9 us -> none
  transfers between devices with their start and end apart: 6 -> 0, of which waited for: 4 -> 0; matrix products, arithmetic and copies ran while one was open for 8% -> 0% of each run, Pallas kernels for 0% -> 0%
where the time goes in v1:
time: 111 us
  Pallas kernels  99.3 us (89%)
  local copies, waits for them, and re-layouts  10.7 us (10%)
    pallas_call x1, Pallas kernels, body(): pl.pallas_call(functools.partial(kernel, ns, nt), out_shape=(jax.ShapeDty...  99.3 us
    unnamed x26, local copies, waits for them, and re-layouts  10.7 us

profile of v1, /device:TPU:1, one launch (start us, length us, event | category | flops | bytes accessed | tf_op | source)
XLA Modules:
  0.0 110.7 jit_solution(6977547908309972429)
XLA Ops:
  0.6 0.0 copy-start.10
  0.6 0.6 copy-done.10
  1.3 0.0 copy-start
  1.3 0.9 copy-done
  2.2 0.0 copy-start.1
  2.2 0.9 copy-done.1
  3.1 0.0 copy-start.2
  3.1 0.8 copy-done.2
  3.9 0.0 copy-start.3
  3.9 0.7 copy-done.3
  4.6 0.0 copy-start.4
  4.6 0.7 copy-done.4
  5.4 0.0 copy-start.5
  5.4 0.7 copy-done.5
  6.1 0.0 copy-start.6
  6.1 0.7 copy-done.6
  6.8 0.0 copy-start.7
  6.8 0.7 copy-done.7
  7.5 0.0 copy-start.8
  7.5 0.7 copy-done.8
  8.2 0.0 copy-start.9
  8.2 0.7 copy-done.9
  8.9 99.3 %astrometric.1 = (f32[5,128]{1,0:T(8,128)S(1)}, f32[1,128]{1,0:T(1,128)S(1)}, f32[256,128]{1,0:T(8,128)S(1)}, f32[16,256]{1,0:T(8,128)S(1)}) custom-call(f32[16,256]{1,0:T(8,128)S(1)} %copy-done.3, f32[16,256]{1,0:T(8,128)S(1)} %copy-done.4, s32[16,256]{1,0:T(8,128)S(1)} %copy-done.5, f32[5,16,256]{2,1,0:T(8,128)S(1)} %copy-done.1, ...), custom_call_target="tpu_custom_call" | custom-call | tf_op jit(solution)/shard_map/astrometric/pallas_call | solution.py:533
  108.3 0.6 copy.19
  108.9 0.5 copy.20
  109.4 0.7 copy.21
  110.1 0.6 copy.22
Async XLA Ops:
  0.6 0.7 copy-start.10
  1.3 0.9 copy-start
  2.2 0.9 copy-start.1
  3.1 0.8 copy-start.2
  3.9 0.7 copy-start.3
  4.6 0.7 copy-start.4
  5.4 0.7 copy-start.5
  6.1 0.7 copy-start.6
  6.8 0.7 copy-start.7
  7.5 0.7 copy-start.8
  8.2 0.7 copy-start.9

commit v2 on v0

v2 whole, which is shorter than its diff:
```python
import functools

import jax
import jax.numpy as jnp
from jax import lax
from jax.experimental import pallas as pl
from jax.experimental.pallas import tpu as pltpu
from jax.sharding import PartitionSpec as P

MESH = pl.DeviceIdType.MESH
F32, BF16 = jnp.float32, jnp.bfloat16
ROWS, SLOT, SRC, KNOTS, LANES = 16, 256, 128, 32, 128
OBS = ROWS * SLOT
SHARD = 8
PAIRS = [(i, j) for i in range(5) for j in range(i + 1)]
TILES = [(i, h) for i in range(2) for h in range(2)]
NT = (((1,), (1,)), ((), ()))
VMEM_LIMIT = 48 * 2**20


def iota(shape, axis):
    return lax.broadcasted_iota(jnp.int32, shape, axis)


def loop(count, step, unroll=1):
    def body(at, carry):
        step(at)
        return carry

    lax.fori_loop(0, count, body, 0, unroll=unroll)


def split(value):
    head = value.astype(BF16).astype(F32)
    return head, value - head


def nt_dot(left, right):
    return lax.dot_general(left, right, NT, preferred_element_type=F32)


def whole(tiles):
    return jnp.concatenate(
        [jnp.concatenate([tiles[i, 0], tiles[i, 1]], axis=1) for i in range(2)], axis=0
    )


def tile(ref, i, h):
    return ref[8 * i : 8 * i + 8, 128 * h : 128 * h + 128]


def along(table, places):
    return jnp.take_along_axis(table, places, axis=1)


def wide(row, rows=8):
    return jnp.broadcast_to(row, (rows, row.shape[-1]))


def choose(rows, order):
    place = iota((8, rows[0].shape[-1]), 0)
    out = wide(rows[order[0]])
    for r in range(1, 8):
        if order[r] != order[r - 1]:
            out = jnp.where(place >= r, wide(rows[order[r]]), out)
    return out


def factor_of(entries):
    low, inv = {}, {}
    for i in range(5):
        for j in range(i + 1):
            rest = entries[i, j]
            for o in range(j):
                rest = rest - low[i, o] * low[j, o]
            if i == j:
                inv[i] = 1.0 / jnp.sqrt(rest)
            else:
                low[i, j] = rest * inv[j]
    return low, inv


def solve_with(low, inv, right):
    forward = []
    for i in range(5):
        rest = right[i]
        for o in range(i):
            rest = rest - low[i, o] * forward[o]
        forward.append(rest * inv[i])
    out = [None] * 5
    for i in reversed(range(5)):
        rest = forward[i]
        for o in range(i + 1, 5):
            rest = rest - low[o, i] * out[o]
        out[i] = rest * inv[i]
    return out


def by_channel(shape):
    lane = iota(shape, 1)
    return 4 * (lane % 32) + lane // 32


def by_knot(shape):
    lane = iota(shape, 1)
    return 32 * (lane % 4) + lane // 4


def band_place(shape):
    lane = iota(shape, 1)
    return iota(shape, 0) + 32 * (lane // 32) + lane % 4


UNROLL = {"design": 1, "hot": 2, "units": 2, "source": 2, "side": 2, "offsets": 2}


class Device:
    def __init__(self, ns, nt, refs):
        self.ns, self.nt = ns, nt
        self.__dict__.update(refs)

    def row(self, at, k):
        return self.rows_s[at, pl.ds(k, 1), :]

    def prepare(self):
        rows_s = self.rows_s
        weight = self.pres[...].astype(F32) * self.wobs[...]
        root = jnp.sqrt(weight)
        u = self.ph[...]
        square = u * u
        cube = square * u
        other = 1.0 - u
        basis = [
            other * other * other / 6.0,
            (3.0 * cube - 6.0 * square + 4.0) / 6.0,
            (-3.0 * cube + 3.0 * square + 3.0 * u + 1.0) / 6.0,
            cube / 6.0,
        ]
        for j in range(4):
            rows_s[j] = basis[j] * root
            rows_s[4 + j] = basis[j]
        rows_s[8] = weight
        rows_s[9] = root
        head, tail = split(weight)
        rows_s[10] = head
        rows_s[11] = tail

    def design(self, out):
        spread = band_place((ROWS, LANES))
        group = (iota((ROWS, LANES), 1) % 32) // 4
        dd, ap = self.dd, self.ap

        def build(k):
            knot = iota((KNOTS, SLOT), 0) - wide(self.kb[pl.ds(k, 1), :], KNOTS)
            share = jnp.zeros((KNOTS, SLOT), F32)
            for j in range(4):
                share = jnp.where(knot == j, wide(self.row(j, k), KNOTS), share)
            for c in range(4):
                value = share * wide(ap[c, pl.ds(k, 1), :], KNOTS)
                head, tail = split(value)
                dd[k, 32 * c : 32 * c + 32, :] = head.astype(BF16)
                dd[k, 128 + 32 * c : 160 + 32 * c, :] = tail.astype(BF16)

        def design_row(k):
            both = dd[k]
            full = nt_dot(both, both)
            build(lax.rem(k + 1, ROWS))
            normal = full[:128, :128] + full[:128, 128:] + full[128:, :128] + full[128:, 128:]
            packed = jnp.zeros((ROWS, LANES), F32)
            for g in range(8):
                part = along(normal[16 * g : 16 * g + 16], (spread + 16 * g) & 127)
                packed = jnp.where(group == g, part, packed)
            out[2 * k] = packed[:8]
            out[2 * k + 1] = packed[8:]

        build(0)
        loop(ROWS, design_row, UNROLL["design"])

    def hot(self):
        def hot_row(k):
            ids = self.cid[pl.ds(k, 1), :]
            hit = iota((256, SLOT), 0) == wide(lax.shift_right_logical(ids, 7), 256)
            self.hot_hi[:, lanes(k)] = jnp.where(hit, 1.0, 0.0).astype(BF16)
            hit = iota((SRC, SLOT), 0) == wide(self.sid[pl.ds(k, 1), :], SRC)
            self.hot_src[:, lanes(k)] = jnp.where(hit, 1.0, 0.0).astype(BF16)

        loop(ROWS, hot_row, UNROLL["hot"])

    def unit_sums(self, out):
        units = self.units

        def unit_row(k):
            low = self.cid[pl.ds(k, 1), :] & 127
            hit = iota((LANES, SLOT), 0) == wide(low, LANES)
            for at in (0, 1):
                value = jnp.where(hit, wide(self.row(10 + at, k), LANES), 0.0)
                units[128 * at : 128 * at + 128, lanes(k)] = value.astype(BF16)

        loop(ROWS, unit_row, UNROLL["units"])
        both = nt_dot(self.hot_hi[...], units[...])
        sums = both[:, :128] + both[:, 128:]
        for s in range(self.ns):
            out[s, 0:8, :] = sums[8 * s : 8 * s + 8]

    def source_normals(self):
        sp, lhs = self.sp, self.lhs

        def source_row(k):
            a = [sp[i, pl.ds(k, 1), :] for i in range(5)]
            parts = []
            for first in (0, 8):
                chosen = (PAIRS + [(4, 4)])[first : first + 8]
                left = choose(a, [p[0] for p in chosen])
                parts.append(left * choose(a, [p[1] for p in chosen]) * wide(self.row(8, k)))
            value = jnp.concatenate(parts, axis=0)
            head, tail = split(value)
            lhs[:16, lanes(k)] = head.astype(BF16)
            lhs[16:, lanes(k)] = tail.astype(BF16)

        loop(ROWS, source_row, UNROLL["source"])
        sums = nt_dot(lhs[...], self.hot_src[...])
        sums = sums[:16] + sums[16:]
        entries = {}
        for at, (i, j) in enumerate(PAIRS):
            entries[i, j] = sums[at : at + 1] + (1.0 if i == j else 0.0)
        low, inv = factor_of(entries)
        keep = [low[i, j] for i, j in PAIRS if i != j] + [inv[i] for i in range(5)]
        for at, value in enumerate(keep):
            self.fac[at : at + 1] = value

    def offsets(self, table):
        head, tail = split(table.T)
        self.cal_t[:128, :] = head.astype(BF16)
        self.cal_t[128:, :] = tail.astype(BF16)

        def offset_row(k):
            got = jnp.dot(self.cal_t[...], self.hot_hi[:, lanes(k)], preferred_element_type=F32)
            got = got[:128] + got[128:]
            hit = iota((LANES, SLOT), 0) == wide(self.cid[pl.ds(k, 1), :] & 127, LANES)
            self.rows_s[13, pl.ds(k, 1), :] = jnp.sum(
                jnp.where(hit, got, 0.0), axis=0, keepdims=True
            )

        loop(ROWS, offset_row, UNROLL["offsets"])

    def remaining(self, table):
        out = {}
        for t in TILES:
            i, h = t
            base = tile(self.kb, i, h)
            model = jnp.zeros((8, LANES), F32)
            for j in range(4):
                sum_c = jnp.zeros((8, LANES), F32)
                for c in range(4):
                    part = along(table[8 * i : 8 * i + 8], base + (32 * c + j))
                    sum_c = sum_c + tile(self.ap.at[c], i, h) * part
                model = model + tile(self.rows_s.at[4 + j], i, h) * sum_c
            out[t] = tile(self.obs, i, h) - model - tile(self.rows_s.at[13], i, h)
        return out

    def less_sources(self, target, params):
        out = {}
        for t in TILES:
            ids = tile(self.sid, *t)
            total = jnp.zeros((8, LANES), F32)
            for i in range(5):
                total = total + tile(self.sp.at[i], *t) * along(wide(params[i]), ids)
            out[t] = target[t] - total
        return out

    def solve_sources(self, target):
        sp, lhs = self.sp, self.lhs
        self.rows_s[12] = self.rows_s[8] * whole(target)

        def side_row(k):
            a = [sp[i, pl.ds(k, 1), :] for i in range(5)]
            value = choose(a, [0, 1, 2, 3, 4, 4, 4, 4]) * wide(self.row(12, k))
            head, tail = split(value)
            lhs[:16, lanes(k)] = jnp.concatenate([head, tail], axis=0).astype(BF16)

        loop(ROWS, side_row, UNROLL["side"])
        sums = nt_dot(lhs[:16, :], self.hot_src[...])
        sums = sums[:8] + sums[8:]
        kept = [self.fac[at : at + 1] for at in range(15)]
        low = dict(zip([p for p in PAIRS if p[0] != p[1]], kept[:10]))
        return solve_with(low, kept[10:], [sums[i : i + 1] for i in range(5)])

    def right_sides(self, resid, out):
        resid = whole(resid)
        head, tail = split(self.rows_s[8] * resid)
        self.rows_s[10] = head
        self.rows_s[11] = tail
        self.unit_sums(out)
        self.attitude_sides(resid, out)

    def attitude_sides(self, resid, out):
        head, tail = split(self.rows_s[9] * resid)
        left = jnp.concatenate([head, tail], axis=0).astype(BF16)
        for k in range(ROWS):
            got = nt_dot(left, self.dd[k])
            got = got[:, :128] + got[:, 128:]
            got = got[k : k + 1] + got[16 + k : 17 + k]
            out[2 * k, 8:9, :] = got
            out[2 * k + 1, 8:9, :] = got

    def unpack(self, packed):
        lane = iota((ROWS, LANES), 1)
        rows = []
        for g in range(8):
            index = iota((ROWS, LANES), 0) + 16 * g
            ahead = (lane - index) & 127
            place = 32 * (ahead // 32) + 4 * g + ahead % 4
            rows.append(jnp.where(ahead % 32 < 4, along(packed, place), 0.0))
        upper = jnp.concatenate(rows, axis=0)
        r_id, c_id = iota((LANES, LANES), 0), iota((LANES, LANES), 1)
        strict = jnp.where(r_id % 32 == c_id % 32, 0.0, upper)
        full = upper + strict.T + jnp.where(r_id == c_id, 1.0, 0.0)
        order = by_knot((LANES, LANES))
        self.matrix[...] = along(along(full, order).T, order)

    def invert(self, blocks):
        matrix = self.matrix
        lane = iota((ROWS, LANES), 1)
        low = iota((ROWS, LANES), 0)
        lines = {s: matrix[16 * s : 16 * s + 16, :] for s in blocks}
        for j in range(ROWS):
            for s in blocks:
                i = 16 * s + j
                line = lines[s]
                column = along(line, jnp.full((ROWS, LANES), i, jnp.int32))
                pivot = 1.0 / wide(column[j : j + 1])
                scaled = jnp.where(lane[:8] == i, pivot, wide(line[j : j + 1]) * pivot)
                scaled = jnp.concatenate([scaled, scaled], axis=0)
                rest = jnp.where(lane == i, 0.0, line) - column * scaled
                lines[s] = jnp.where(low == j, scaled, rest)
        zeros = jnp.zeros((ROWS, LANES), F32)
        inner = jnp.concatenate([lines.get(s, zeros) for s in range(8)], axis=0)
        moved = jnp.dot(
            matrix[...], inner, precision=lax.Precision.HIGHEST, preferred_element_type=F32
        )
        kept = jnp.ones((ROWS, LANES), F32)
        for s in blocks:
            kept = jnp.where(lane // 16 == s, 0.0, kept)
        for s in range(8):
            rows = slice(16 * s, 16 * s + 16)
            if s in blocks:
                matrix[rows, :] = lines[s]
            else:
                matrix[rows, :] = matrix[rows, :] * kept - moved[rows]

    def advance(self, got, later, offsets, q):
        later[0:8, :] = offsets + got[0:8] * self.inv_den[...]
        step = jnp.dot(
            along(wide(got[8:9]), by_knot((8, LANES))),
            self.matrix[...],
            precision=lax.Precision.HIGHEST,
            preferred_element_type=F32,
        )
        later[8:9, :] = q + along(step, by_channel((8, LANES)))[0:1]


INPUTS = ["obs", "wobs", "pres", "sp", "ap", "ph", "kb", "sid", "cid", "att", "cal"]
OUTPUTS = ["params_o", "att_o", "cal_o", "res_o"]


def shapes(ns, nt):
    shard = SHARD + 1
    vmem = lambda *shape: pltpu.VMEM(shape, F32)
    out = {
        "rows_s": vmem(14, ROWS, SLOT),
        "dd": pltpu.VMEM((ROWS, 256, SLOT), BF16),
        "hot_hi": pltpu.VMEM((256, OBS), BF16),
        "hot_src": pltpu.VMEM((SRC, OBS), BF16),
        "units": pltpu.VMEM((256, OBS), BF16),
        "lhs": pltpu.VMEM((32, OBS), BF16),
        "cal_t": pltpu.VMEM((256, 256), BF16),
        "matrix": vmem(LANES, LANES),
        "fac": vmem(16, LANES),
        "inv_den": vmem(8, LANES),
        "qbuf": vmem(nt, 1, LANES),
        "qsend": vmem(1, LANES),
        "ns_s": vmem(ns, 8, LANES),
        "ns_r": vmem(ns, 8, LANES),
        "nt_s": vmem(8, LANES),
        "nt_r": vmem(nt, 8, LANES),
        "ws_s": vmem(ns, 8, LANES),
        "ws_r": vmem(ns, 8, LANES),
        "wt_s": vmem(8, LANES),
        "wt_r": vmem(nt, 8, LANES),
        "pair_r": vmem(2, 8, LANES),
    }
    for n in (2, 3):
        out[f"a{n}s"] = vmem(ns, shard, LANES)
        out[f"a{n}r"] = vmem(ns, shard, LANES)
        out[f"b{n}s"] = vmem(shard, LANES)
        out[f"b{n}r"] = vmem(nt, shard, LANES)
        out[f"c{n}s"] = vmem(shard, LANES)
        out[f"c{n}r"] = vmem(ns, shard, LANES)
    return out


def lanes(k):
    return pl.ds(pl.multiple_of(k * SLOT, SLOT), SLOT)


def ring_order(count):
    return sorted(range(1, count), key=lambda o: -min(o, count - o))


def plane_order(ns):
    far = (0, 1, 2, 1)
    every = [(y, x, c) for y in range(4) for x in range(4) for c in range(ns // 16)]
    return sorted(every, key=lambda o: -4 * (far[o[0]] + far[o[1]]) - o[2])[:-1]


def kernel(ns, nt, *refs):
    count = len(INPUTS)
    given = dict(zip(INPUTS, refs[:count]))
    results = dict(zip(OUTPUTS, refs[count : count + 4]))
    scratch = refs[count + 4 :]
    names = list(shapes(ns, nt))
    d = Device(ns, nt, dict(zip(names, scratch)))
    local = dict(zip(INPUTS, scratch[len(names) : len(names) + count]))
    d.__dict__.update(local)
    send, recv, load = scratch[len(names) + count :]
    me_s, me_t = lax.axis_index("src"), lax.axis_index("tm")
    my_y, my_x, my_c = me_s // 8, lax.rem(me_s // 2, 4), lax.rem(me_s, 2)

    def fetch(name):
        at = INPUTS.index(name)
        return pltpu.make_async_copy(given[name], local[name], load.at[at])

    def ready(*wanted):
        for name in wanted:
            fetch(name).wait()

    in_plane = [
        lax.rem(my_y + y, 4) * 8 + lax.rem(my_x + x, 4) * 2 + lax.rem(my_c + c, 2)
        for y, x, c in plane_order(ns)
    ]
    in_ring = [lax.rem(me_t + o, nt) for o in ring_order(nt)]

    def partners(axis, step):
        for other in in_plane if axis == "src" else in_ring:
            step(other)

    def partners_loop(axis, step):
        size, me = (ns, me_s) if axis == "src" else (nt, me_t)
        loop(size - 1, lambda at: step(lax.rem(me + 1 + at, size)))

    class Exchange:
        def __init__(self, stage, axis, source, target, shards=False):
            self.stage, self.axis, self.source, self.target = stage, axis, source, target
            self.me = me_s if axis == "src" else me_t
            self.shards = shards

        def copy(self, other, slot, sender):
            return pltpu.make_async_remote_copy(
                src_ref=self.source.at[other] if self.shards else self.source,
                dst_ref=self.target.at[slot],
                send_sem=send.at[self.stage, other],
                recv_sem=recv.at[self.stage, sender],
                device_id=(other, me_t) if self.axis == "src" else (me_s, other),
                device_id_type=MESH,
            )

        def start(self):
            partners(self.axis, lambda o: self.copy(o, self.me, self.me).start())
            self.target[self.me] = self.source[self.me] if self.shards else self.source[...]

        def wait(self):
            partners_loop(self.axis, lambda o: self.copy(o, o, o).wait_recv())

        def sent(self):
            partners_loop(self.axis, lambda o: self.copy(o, self.me, self.me).wait_send())

        def total(self):
            return jnp.sum(self.target[...], axis=0)

    barrier = pltpu.get_barrier_semaphore()

    def greet_src(o):
        pl.semaphore_signal(barrier, inc=1, device_id=(o, me_t), device_id_type=MESH)

    def greet_tm(o):
        pl.semaphore_signal(barrier, inc=1, device_id=(me_s, o), device_id_type=MESH)

    partners("tm", greet_tm)
    for name in ("wobs", "pres", "ph", "kb", "ap", "att", "cid", "sid", "sp", "cal", "obs"):
        fetch(name).start()
    partners("src", greet_src)

    first_q = Exchange(0, "tm", d.qsend, d.qbuf)
    normals_s = Exchange(1, "src", d.ns_s, d.ns_r, shards=True)
    normals_t = Exchange(2, "tm", d.nt_s, d.nt_r)
    weights_s = Exchange(3, "src", d.ws_s, d.ws_r, shards=True)
    weights_t = Exchange(4, "tm", d.wt_s, d.wt_r)

    ready("wobs", "pres", "ph")
    d.prepare()
    ready("kb", "ap")
    d.design(d.ns_s)
    ready("att")
    d.qsend[...] = along(wide(d.att[...]), by_channel((8, LANES)))[0:1]

    pl.semaphore_wait(barrier, ns + nt - 2)
    first_q.start()
    normals_s.start()
    ready("cid", "sid")
    d.hot()
    d.unit_sums(d.ws_s)
    weights_s.start()
    ready("sp")
    d.source_normals()
    ready("cal", "obs")
    d.offsets(d.cal[...])
    normals_s.wait()
    d.nt_s[...] = normals_s.total()
    normals_t.start()
    weights_s.wait()
    d.wt_s[...] = weights_s.total()
    weights_t.start()

    def reduce(n):
        at = 5 + 3 * (n - 2)
        return (
            Exchange(at, "src", getattr(d, f"a{n}s"), getattr(d, f"a{n}r"), shards=True),
            Exchange(at + 1, "tm", getattr(d, f"b{n}s"), getattr(d, f"b{n}r")),
            Exchange(at + 2, "src", getattr(d, f"c{n}s"), getattr(d, f"c{n}r")),
        )

    over_src, over_tm, back = reduce(2)
    first_q.wait()
    table = jnp.concatenate([d.qbuf[k] for k in range(nt)], axis=0)
    target = d.remaining(table)
    params = d.solve_sources(target)
    d.right_sides(d.less_sources(target, params), d.a2s)
    over_src.start()

    normals_t.wait()
    half = my_c
    owned = me_s // 2
    d.pair_r[half] = normals_t.total()
    swap = pltpu.make_async_remote_copy(
        src_ref=d.pair_r.at[half],
        dst_ref=d.pair_r.at[half],
        send_sem=send.at[11, 0],
        recv_sem=recv.at[11, 0],
        device_id=(me_s + 1 - 2 * half, me_t),
        device_id_type=MESH,
    )
    swap.start()
    first_q.sent()
    normals_s.sent()
    swap.wait()
    d.unpack(jnp.concatenate([d.pair_r[0], d.pair_r[1]], axis=0))
    d.invert((1, 3, 5, 7))

    over_src.wait()
    d.b2s[...] = over_src.total()
    over_tm.start()
    d.invert((2, 6))
    d.invert((4,))
    d.invert((0,))
    weights_t.wait()
    d.inv_den[...] = 1.0 / (1.0 + weights_t.total())
    weights_s.sent()
    normals_t.sent()
    weights_t.sent()
    over_src.sent()

    own_cal = pl.ds(pl.multiple_of(8 * me_s, 8), 8)
    over_tm.wait()
    d.advance(over_tm.total(), d.c2s, d.cal[own_cal, :], d.qbuf[owned])
    back.start()
    over_tm.sent()
    back.wait()

    def tables_of(got):
        knots = jnp.concatenate([got[2 * k, 8:9, :] for k in range(nt)], axis=0)
        return knots, got[:, 0:8, :].reshape(ns * 8, LANES)

    table, cal = tables_of(d.c2r)
    d.offsets(cal)
    target = d.remaining(table)
    params = d.solve_sources(target)
    d.right_sides(d.less_sources(target, params), d.a3s)
    back.sent()
    over_src, over_tm, back = reduce(3)
    over_src.start()
    for i in range(5):
        results["params_o"][i : i + 1, :] = params[i]
    over_src.wait()
    d.b3s[...] = over_src.total()
    over_tm.start()
    over_src.sent()
    over_tm.wait()
    d.advance(over_tm.total(), d.c3s, d.c2s[0:8, :], d.c2s[8:9, :])
    back.start()
    over_tm.sent()
    back.wait()

    table, cal = tables_of(d.c3r)
    results["cal_o"][...] = cal
    d.offsets(cal)
    results["res_o"][...] = whole(d.less_sources(d.remaining(table), params))
    results["att_o"][...] = along(wide(d.c3r[2 * me_t, 8:9, :]), by_knot((8, LANES)))[0:1]
    back.sent()


def body(ns, nt, *arrays):
    *arrays, attitude, calibration = arrays
    arrays = [*arrays, attitude.reshape(1, LANES), calibration.reshape(256, LANES)]
    arrays = [pltpu.with_memory_space_constraint(x, pltpu.HBM) for x in arrays]
    vmem = pl.BlockSpec(memory_space=pltpu.VMEM)
    params, att, cal, resid = pl.pallas_call(
        functools.partial(kernel, ns, nt),
        out_shape=(
            jax.ShapeDtypeStruct((5, SRC), F32),
            jax.ShapeDtypeStruct((1, LANES), F32),
            jax.ShapeDtypeStruct((256, LANES), F32),
            jax.ShapeDtypeStruct((ROWS, SLOT), F32),
        ),
        in_specs=[pl.BlockSpec(memory_space=pltpu.HBM)] * len(arrays),
        out_specs=(vmem,) * 4,
        scratch_shapes=[
            *shapes(ns, nt).values(),
            *(pltpu.VMEM(x.shape, x.dtype) for x in arrays),
            pltpu.SemaphoreType.DMA((12, ns)),
            pltpu.SemaphoreType.DMA((12, ns)),
            pltpu.SemaphoreType.DMA((len(arrays),)),
        ],
        compiler_params=pltpu.CompilerParams(
            collective_id=0, has_side_effects=True, vmem_limit_bytes=VMEM_LIMIT
        ),
        name="astrometric",
    )(*arrays)
    return params, att.reshape(LANES), cal.reshape(-1), resid


def solution(mesh):
    spread = P(None, ("src", "tm"))
    return jax.shard_map(
        functools.partial(body, mesh.shape["src"], mesh.shape["tm"]),
        mesh=mesh,
        in_specs=(
            spread,
            spread,
            spread,
            P(None, None, ("src", "tm")),
            P(None, None, ("src", "tm")),
            spread,
            spread,
            spread,
            spread,
            P("tm"),
            P(),
        ),
        out_specs=(spread, P("tm"), P(), spread),
        check_vma=False,
    )
```

time: 1530 us -> 85.5 us (0.06)
  waiting for transfers between devices: 938 us -> 0 us
  blocking collectives: 271 us -> 0 us
  local copies, waits for them, and re-layouts: 134 us -> 2.37 us
  other arithmetic: 123 us -> 0 us
  Pallas kernels: 0 us -> 82.2 us
  matrix products: 28.4 us -> 0 us
  between operations: 16.6 us -> 0.64 us
    psum x4 -> x0, waiting for transfers between devices: 938 us -> none  [the longest x2 740 us: body(): numer, denom = lax.psum((numer, denom), ('src', 'tm'))]
    psum x2 -> x0, blocking collectives: 151 us -> none  [body(): normal, right = lax.psum((normal[0], right[0]), 'src')]
    pallas_call x0 -> x1, Pallas kernels: none -> 82.2 us  [body(): pl.pallas_call(functools.partial(kernel, ns, nt), out_shape=(jax.ShapeDty...]
    all_gather x3 -> x0, blocking collectives: 74.3 us -> none  [attitude_model(): coefficients = lax.all_gather(local, 'tm', axis=0, tiled=True)]
    gather x6 -> x0, local copies, waits for them, and re-layouts: 69.1 us -> none  [the longest x4 46.1 us: body(): cal_now[cal_id]]
    scatter-add x3 -> x0, other arithmetic: 67.6 us -> none  [the longest x2 45 us: body(): jax.ops.segment_sum((weighted * resid).reshape(-1), flat_cal, num_segment...]
    dynamic_slice x128 -> x0, local copies, waits for them, and re-layouts: 47.2 us -> none  [the longest x96 46.8 us: source_solve(): lax.scan(accumulate, jnp.zeros((len(products), count), jnp.float32), (sta...]
    unnamed x2 -> x0, blocking collectives: 45.9 us -> none
  transfers between devices with their start and end apart: 6 -> 0, of which waited for: 4 -> 0; matrix products, arithmetic and copies ran while one was open for 8% -> 0% of each run, Pallas kernels for 0% -> 0%
where the time goes in v2:
time: 85.5 us; the launch traced here: 85.3 us
  Pallas kernels  82.2 us (96%)
  local copies, waits for them, and re-layouts  2.37 us (3%)
    pallas_call x1, Pallas kernels, body(): pl.pallas_call(functools.partial(kernel, ns, nt), out_shape=(jax.ShapeDty...  82.2 us
    unnamed x4, local copies, waits for them, and re-layouts  2.37 us

profile of v2, /device:TPU:1, one launch (start us, length us, event | category | flops | bytes accessed | tf_op | source)
XLA Modules:
  0.0 85.3 jit_solution(12140442027918644465)
XLA Ops:
  0.6 82.2 %astrometric.1 = (f32[5,128]{1,0:T(8,128)S(1)}, f32[1,128]{1,0:T(1,128)S(1)}, f32[256,128]{1,0:T(8,128)S(1)}, f32[16,256]{1,0:T(8,128)S(1)}) custom-call(f32[16,256]{1,0:T(8,128)} %refs_0_.1, f32[16,256]{1,0:T(8,128)} %refs_1_.1, s32[16,256]{1,0:T(8,128)} %refs_2_.1, f32[5,16,256]{2,1,0:T(8,128)} %refs_3_.1, f32[4,16,256]{2,1,0:T(8,128)} %refs_4_.1, ...), custom_call_target="tpu_custom_call" | custom-call | tf_op jit(solution)/shard_map/astrometric/pallas_call | solution.py:616
  82.9 0.6 copy.19
  83.5 0.5 copy.20
  84.0 0.7 copy.21
  84.7 0.6 copy.22

commit v3 on v2

--- a/solution.py
+++ b/solution.py
@@ -111,7 +111,7 @@
     return iota(shape, 0) + 32 * (lane // 32) + lane % 4
 
 
-UNROLL = {"design": 1, "hot": 2, "units": 2, "source": 2, "side": 2, "offsets": 2}
+UNROLL = {"design": 16, "hot": 16, "units": 16, "source": 16, "side": 16, "offsets": 16}
 
 
 class Device:
@@ -608,6 +608,28 @@
     back.sent()
 
 
+def publish(*arrays):
+    def copy(*refs):
+        *refs, load = refs
+        count = len(refs) // 2
+        copies = [
+            pltpu.make_async_copy(refs[at], refs[count + at], load.at[at]) for at in range(count)
+        ]
+        for each in copies:
+            each.start()
+        for each in copies:
+            each.wait()
+
+    return pl.pallas_call(
+        copy,
+        out_shape=tuple(jax.ShapeDtypeStruct(x.shape, x.dtype) for x in arrays),
+        in_specs=[pl.BlockSpec(memory_space=pltpu.VMEM)] * len(arrays),
+        out_specs=(pl.BlockSpec(memory_space=pltpu.HBM),) * len(arrays),
+        scratch_shapes=[pltpu.SemaphoreType.DMA((len(arrays),))],
+        name="publish",
+    )(*arrays)
+
+
 def body(ns, nt, *arrays):
     *arrays, attitude, calibration = arrays
     arrays = [*arrays, attitude.reshape(1, LANES), calibration.reshape(256, LANES)]
@@ -616,10 +638,10 @@
     params, att, cal, resid = pl.pallas_call(
         functools.partial(kernel, ns, nt),
         out_shape=(
-            jax.ShapeDtypeStruct((5, SRC), F32),
-            jax.ShapeDtypeStruct((1, LANES), F32),
-            jax.ShapeDtypeStruct((256, LANES), F32),
-            jax.ShapeDtypeStruct((ROWS, SLOT), F32),
+            pltpu.VMEM((5, SRC), F32),
+            pltpu.VMEM((1, LANES), F32),
+            pltpu.VMEM((256, LANES), F32),
+            pltpu.VMEM((ROWS, SLOT), F32),
         ),
         in_specs=[pl.BlockSpec(memory_space=pltpu.HBM)] * len(arrays),
         out_specs=(vmem,) * 4,
@@ -635,6 +657,8 @@
         ),
         name="astrometric",
     )(*arrays)
+    held = [pltpu.with_memory_space_constraint(x, pltpu.VMEM) for x in (params, att, cal, resid)]
+    params, att, cal, resid = publish(*held)
     return params, att.reshape(LANES), cal.reshape(-1), resid
 
 

time: 85.5 us -> 75.5 us (0.88)
  Pallas kernels: 82.2 us -> 74.5 us
  local copies, waits for them, and re-layouts: 2.37 us -> 0 us
    pallas_call x1 -> x2, Pallas kernels: 82.2 us -> 74.5 us  [the longest x1 73.8 us: body(): pl.pallas_call(functools.partial(kernel, ns, nt), out_shape=(pltpu.VMEM((...]
    unnamed x4 -> x0, local copies, waits for them, and re-layouts: 2.37 us -> none
where the time goes in v3:
time: 75.5 us; the launch traced here: 75.3 us
  Pallas kernels  74.5 us (99%)
  between operations  0.8 us (1%)
    pallas_call x1, Pallas kernels, body(): pl.pallas_call(functools.partial(kernel, ns, nt), out_shape=(pltpu.VMEM((...  73.8 us

profile of v3, /device:TPU:1, one launch (start us, length us, event | category | flops | bytes accessed | tf_op | source)
XLA Modules:
  0.0 75.3 jit_solution(17461401713722024983)
XLA Ops:
  0.6 73.8 %astrometric.1 = (f32[5,128]{1,0:T(8,128)S(1)}, f32[1,128]{1,0:T(1,128)S(1)}, f32[256,128]{1,0:T(8,128)S(1)}, f32[16,256]{1,0:T(8,128)S(1)}) custom-call(f32[16,256]{1,0:T(8,128)} %refs_0_.1, f32[16,256]{1,0:T(8,128)} %refs_1_.1, s32[16,256]{1,0:T(8,128)} %refs_2_.1, f32[5,16,256]{2,1,0:T(8,128)} %refs_3_.1, f32[4,16,256]{2,1,0:T(8,128)} %refs_4_.1, ...), custom_call_target="tpu_custom_call" | custom-call | tf_op jit(solution)/shard_map/astrometric/pallas_call | solution.py:638
  74.5 0.7 publish.1

commit v4 on v3

--- a/solution.py
+++ b/solution.py
@@ -207,6 +207,7 @@
 
         def source_row(k):
             a = [sp[i, pl.ds(k, 1), :] for i in range(5)]
+            self.tiles_a[k] = choose(a, [0, 1, 2, 3, 4, 4, 4, 4])
             parts = []
             for first in (0, 8):
                 chosen = (PAIRS + [(4, 4)])[first : first + 8]
@@ -243,7 +244,7 @@
 
         loop(ROWS, offset_row, UNROLL["offsets"])
 
-    def remaining(self, table):
+    def remaining(self, table, start):
         out = {}
         for t in TILES:
             i, h = t
@@ -255,7 +256,7 @@
                     part = along(table[8 * i : 8 * i + 8], base + (32 * c + j))
                     sum_c = sum_c + tile(self.ap.at[c], i, h) * part
                 model = model + tile(self.rows_s.at[4 + j], i, h) * sum_c
-            out[t] = tile(self.obs, i, h) - model - tile(self.rows_s.at[13], i, h)
+            out[t] = start[t] - model - tile(self.rows_s.at[13], i, h)
         return out
 
     def less_sources(self, target, params):
@@ -269,12 +270,11 @@
         return out
 
     def solve_sources(self, target):
-        sp, lhs = self.sp, self.lhs
+        lhs = self.lhs
         self.rows_s[12] = self.rows_s[8] * whole(target)
 
         def side_row(k):
-            a = [sp[i, pl.ds(k, 1), :] for i in range(5)]
-            value = choose(a, [0, 1, 2, 3, 4, 4, 4, 4]) * wide(self.row(12, k))
+            value = self.tiles_a[k] * wide(self.row(12, k))
             head, tail = split(value)
             lhs[:16, lanes(k)] = jnp.concatenate([head, tail], axis=0).astype(BF16)
 
@@ -323,16 +323,25 @@
         lane = iota((ROWS, LANES), 1)
         low = iota((ROWS, LANES), 0)
         lines = {s: matrix[16 * s : 16 * s + 16, :] for s in blocks}
-        for j in range(ROWS):
+        for j in range(0, ROWS, 2):
             for s in blocks:
                 i = 16 * s + j
                 line = lines[s]
-                column = along(line, jnp.full((ROWS, LANES), i, jnp.int32))
-                pivot = 1.0 / wide(column[j : j + 1])
-                scaled = jnp.where(lane[:8] == i, pivot, wide(line[j : j + 1]) * pivot)
-                scaled = jnp.concatenate([scaled, scaled], axis=0)
-                rest = jnp.where(lane == i, 0.0, line) - column * scaled
-                lines[s] = jnp.where(low == j, scaled, rest)
+                first = along(line, jnp.full((ROWS, LANES), i, jnp.int32))
+                second = along(line, jnp.full((ROWS, LANES), i + 1, jnp.int32))
+                top, side = wide(first[j : j + 1]), wide(first[j + 1 : j + 2])
+                end = wide(second[j + 1 : j + 2])
+                scale = 1.0 / (top * end - side * side)
+                here, there = lane[:8] == i, lane[:8] == i + 1
+                upper = jnp.where(here, 1.0, jnp.where(there, 0.0, wide(line[j : j + 1])))
+                under = jnp.where(here, 0.0, jnp.where(there, 1.0, wide(line[j + 1 : j + 2])))
+                above = (end * upper - side * under) * scale
+                below = (top * under - side * upper) * scale
+                above = jnp.concatenate([above, above], axis=0)
+                below = jnp.concatenate([below, below], axis=0)
+                rest = jnp.where((lane == i) | (lane == i + 1), 0.0, line)
+                rest = rest - first * above - second * below
+                lines[s] = jnp.where(low == j, above, jnp.where(low == j + 1, below, rest))
         zeros = jnp.zeros((ROWS, LANES), F32)
         inner = jnp.concatenate([lines.get(s, zeros) for s in range(8)], axis=0)
         moved = jnp.dot(
@@ -348,14 +357,27 @@
             else:
                 matrix[rows, :] = matrix[rows, :] * kept - moved[rows]
 
+    def split_inverse(self):
+        rest = self.matrix[...]
+        for at in range(3):
+            head = rest.astype(BF16)
+            self.terms[:, 128 * at : 128 * at + 128] = head
+            rest = rest - head.astype(F32)
+
     def advance(self, got, later, offsets, q):
         later[0:8, :] = offsets + got[0:8] * self.inv_den[...]
-        step = jnp.dot(
-            along(wide(got[8:9]), by_knot((8, LANES))),
-            self.matrix[...],
-            precision=lax.Precision.HIGHEST,
-            preferred_element_type=F32,
+        right = along(wide(got[8:9]), by_knot((8, LANES)))
+        head, rest = split(right)
+        middle, tail = split(rest)
+        place = iota((8, LANES), 0)
+        left = jnp.where(place == 0, head, jnp.where(place == 1, middle, tail))
+        left = jnp.concatenate([left, jnp.zeros((8, LANES), F32)], axis=0).astype(BF16)
+        every = jnp.dot(left, self.terms[...], preferred_element_type=F32)
+        step = every[0:1, 0:128] + (
+            (every[0:1, 128:256] + every[1:2, 0:128])
+            + (every[0:1, 256:384] + every[1:2, 128:256] + every[2:3, 0:128])
         )
+        step = wide(step)
         later[8:9, :] = q + along(step, by_channel((8, LANES)))[0:1]
 
 
@@ -375,6 +397,8 @@
         "lhs": pltpu.VMEM((32, OBS), BF16),
         "cal_t": pltpu.VMEM((256, 256), BF16),
         "matrix": vmem(LANES, LANES),
+        "tiles_a": vmem(ROWS, 8, SLOT),
+        "terms": pltpu.VMEM((LANES, 3 * LANES), BF16),
         "fac": vmem(16, LANES),
         "inv_den": vmem(8, LANES),
         "qbuf": vmem(nt, 1, LANES),
@@ -532,7 +556,7 @@
     over_src, over_tm, back = reduce(2)
     first_q.wait()
     table = jnp.concatenate([d.qbuf[k] for k in range(nt)], axis=0)
-    target = d.remaining(table)
+    target = d.remaining(table, {t: tile(d.obs, *t) for t in TILES})
     params = d.solve_sources(target)
     d.right_sides(d.less_sources(target, params), d.a2s)
     over_src.start()
@@ -552,16 +576,16 @@
     swap.start()
     first_q.sent()
     normals_s.sent()
+    over_src.wait()
+    d.b2s[...] = over_src.total()
+    over_tm.start()
     swap.wait()
     d.unpack(jnp.concatenate([d.pair_r[0], d.pair_r[1]], axis=0))
     d.invert((1, 3, 5, 7))
-
-    over_src.wait()
-    d.b2s[...] = over_src.total()
-    over_tm.start()
     d.invert((2, 6))
     d.invert((4,))
     d.invert((0,))
+    d.split_inverse()
     weights_t.wait()
     d.inv_den[...] = 1.0 / (1.0 + weights_t.total())
     weights_s.sent()
@@ -582,7 +606,7 @@
 
     table, cal = tables_of(d.c2r)
     d.offsets(cal)
-    target = d.remaining(table)
+    target = d.remaining(table, {t: tile(d.obs, *t) for t in TILES})
     params = d.solve_sources(target)
     d.right_sides(d.less_sources(target, params), d.a3s)
     back.sent()
@@ -593,6 +617,7 @@
     over_src.wait()
     d.b3s[...] = over_src.total()
     over_tm.start()
+    left = d.less_sources({t: tile(d.obs, *t) for t in TILES}, params)
     over_src.sent()
     over_tm.wait()
     d.advance(over_tm.total(), d.c3s, d.c2s[0:8, :], d.c2s[8:9, :])
@@ -603,7 +628,7 @@
     table, cal = tables_of(d.c3r)
     results["cal_o"][...] = cal
     d.offsets(cal)
-    results["res_o"][...] = whole(d.less_sources(d.remaining(table), params))
+    results["res_o"][...] = whole(d.remaining(table, left))
     results["att_o"][...] = along(wide(d.c3r[2 * me_t, 8:9, :]), by_knot((8, LANES)))[0:1]
     back.sent()
 

time: 75.5 us -> 75.6 us (level)
  no operation moved by 1% of the time
where the time goes in v4:
time: 75.6 us; the launch traced here: 75.4 us
  Pallas kernels  74.6 us (99%)
  between operations  0.8 us (1%)
    pallas_call x1, Pallas kernels, body(): pl.pallas_call(functools.partial(kernel, ns, nt), out_shape=(pltpu.VMEM((...  73.9 us

profile of v4, /device:TPU:1, one launch (start us, length us, event | category | flops | bytes accessed | tf_op | source)
XLA Modules:
  0.0 75.4 jit_solution(4029602399966840241)
XLA Ops:
  0.6 73.9 %astrometric.1 = (f32[5,128]{1,0:T(8,128)S(1)}, f32[1,128]{1,0:T(1,128)S(1)}, f32[256,128]{1,0:T(8,128)S(1)}, f32[16,256]{1,0:T(8,128)S(1)}) custom-call(f32[16,256]{1,0:T(8,128)} %refs_0_.1, f32[16,256]{1,0:T(8,128)} %refs_1_.1, s32[16,256]{1,0:T(8,128)} %refs_2_.1, f32[5,16,256]{2,1,0:T(8,128)} %refs_3_.1, f32[4,16,256]{2,1,0:T(8,128)} %refs_4_.1, ...), custom_call_target="tpu_custom_call" | custom-call | tf_op jit(solution)/shard_map/astrometric/pallas_call | solution.py:663
  74.6 0.7 publish.1

commit v5 on v4

--- a/solution.py
+++ b/solution.py
@@ -541,9 +541,6 @@
     normals_s.wait()
     d.nt_s[...] = normals_s.total()
     normals_t.start()
-    weights_s.wait()
-    d.wt_s[...] = weights_s.total()
-    weights_t.start()
 
     def reduce(n):
         at = 5 + 3 * (n - 2)
@@ -560,6 +557,9 @@
     params = d.solve_sources(target)
     d.right_sides(d.less_sources(target, params), d.a2s)
     over_src.start()
+    weights_s.wait()
+    d.wt_s[...] = weights_s.total()
+    weights_t.start()
 
     normals_t.wait()
     half = my_c
@@ -609,9 +609,10 @@
     target = d.remaining(table, {t: tile(d.obs, *t) for t in TILES})
     params = d.solve_sources(target)
     d.right_sides(d.less_sources(target, params), d.a3s)
-    back.sent()
+    returned = back
     over_src, over_tm, back = reduce(3)
     over_src.start()
+    returned.sent()
     for i in range(5):
         results["params_o"][i : i + 1, :] = params[i]
     over_src.wait()

time: 75.6 us -> 73.3 us (0.970)
  Pallas kernels: 74.6 us -> 72.3 us
    pallas_call x1, Pallas kernels: 73.9 us -> 71.6 us  [body(): pl.pallas_call(functools.partial(kernel, ns, nt), out_shape=(pltpu.VMEM((...]
where the time goes in v5:
time: 73.3 us; the launch traced here: 73.1 us
  Pallas kernels  72.3 us (99%)
  between operations  0.8 us (1%)
    pallas_call x1, Pallas kernels, body(): pl.pallas_call(functools.partial(kernel, ns, nt), out_shape=(pltpu.VMEM((...  71.6 us

profile of v5, /device:TPU:1, one launch (start us, length us, event | category | flops | bytes accessed | tf_op | source)
XLA Modules:
  0.0 73.1 jit_solution(15911196913546121946)
XLA Ops:
  0.6 71.6 %astrometric.1 = (f32[5,128]{1,0:T(8,128)S(1)}, f32[1,128]{1,0:T(1,128)S(1)}, f32[256,128]{1,0:T(8,128)S(1)}, f32[16,256]{1,0:T(8,128)S(1)}) custom-call(f32[16,256]{1,0:T(8,128)} %refs_0_.1, f32[16,256]{1,0:T(8,128)} %refs_1_.1, s32[16,256]{1,0:T(8,128)} %refs_2_.1, f32[5,16,256]{2,1,0:T(8,128)} %refs_3_.1, f32[4,16,256]{2,1,0:T(8,128)} %refs_4_.1, ...), custom_call_target="tpu_custom_call" | custom-call | tf_op jit(solution)/shard_map/astrometric/pallas_call | solution.py:664
  72.3 0.7 publish.1
